TPU v7x, 32 devices: a whole 2x2x4 slice. The times are simulated.
32 devices in a mesh: groups: 2 (over x), wide: 16 (over z, y, core).
Axes of the slice: x: 2, y: 2, z: 4, core: 2. Of those that a mesh axis runs over, the one named last changes fastest.
Arguments:
- features: float32 [196608, 64], P(('groups', 'wide')), parts along dimension 0, may hold values from -6 to 6
- targets: float32 [196608, 128], P(('groups', 'wide')), parts along dimension 0, may hold values from -6 to 6
- block_ids: int32 [4], P('groups'), parts along dimension 0, may hold values from 0 to 95
- order: int32 [196608], P(('groups', 'wide')), parts along dimension 0, may hold values from 0 to 6143, as said below
Outputs:
- coeffs: float32 [196608, 128], P(('groups', 'wide')), parts along dimension 0
- residual: float32 [196608, 128], P(('groups', 'wide')), parts along dimension 0
There are 2 independent parts, one for each index of `groups`. A program takes and returns all parts, laid end to end along the dimension named above; each array names one. Nothing has to cross between parts.
Inputs may be any that keep to these rules, and one draw needn't show every extreme that they name: `order`: each aligned block of 6144 entries starting at a multiple of 6144 is a permutation of 0 .. 6143.
All inputs are finite; a program needn't handle non-finite values.
Results may differ from a plain program's by a relative error of at most 0.0003.
Values sent between devices are 32-bit elements; how exact they have to be, the bound alone decides.
A program may use at most 128 MiB of HBM per device.

v0:
```python
import jax
import jax.numpy as jnp
from jax import lax
from jax.sharding import PartitionSpec as P

BLOCK = 1024
STEPS = 2


def kernel(left, right):
    sq_left = jnp.sum(left * left, axis=1)
    sq_right = jnp.sum(right * right, axis=1)
    cross = jnp.dot(
        left, right.T, precision=lax.Precision.HIGHEST, preferred_element_type=jnp.float32
    )
    return jnp.exp(-(sq_left[:, None] + sq_right[None, :] - 2.0 * cross) / 32.0)


def factorize(gram):
    half = gram.shape[0] // 2
    top = jnp.linalg.cholesky(gram[:half, :half])
    lower_left = lax.linalg.triangular_solve(
        top, gram[half:, :half], left_side=False, lower=True, transpose_a=True
    )
    schur = gram[half:, half:] - jnp.dot(
        lower_left,
        lower_left.T,
        precision=lax.Precision.HIGHEST,
        preferred_element_type=jnp.float32,
    )
    bottom = jnp.linalg.cholesky(schur)
    upper_row = jnp.concatenate([top, jnp.zeros((half, half), dtype=gram.dtype)], axis=1)
    lower_row = jnp.concatenate([lower_left, bottom], axis=1)
    return jnp.concatenate([upper_row, lower_row], axis=0)


def solve_with(factor, right_side):
    halfway = lax.linalg.triangular_solve(factor, right_side, left_side=True, lower=True)
    return lax.linalg.triangular_solve(
        factor, halfway, left_side=True, lower=True, transpose_a=True
    )


def body(features, targets, block_ids, order):
    shards = lax.axis_size("wide")
    me_index = lax.axis_index("wide")
    per = BLOCK // shards
    coeffs = jnp.zeros_like(targets)
    residual = targets
    all_local = []
    for step in range(STEPS):
        start = block_ids[step] * per
        all_local.append(lax.dynamic_slice_in_dim(order, start, per, 0))
    for step in range(STEPS):
        local = all_local[step]
        block_x, block_r = (
            lax.all_gather(features[local], "wide", axis=0, tiled=True),
            lax.all_gather(residual[local], "wide", axis=0, tiled=True),
        )
        gram = kernel(block_x, block_x) + 1.0 * jnp.eye(BLOCK, dtype=jnp.float32)
        factor = factorize(gram)
        delta = solve_with(factor, block_r)
        own = lax.dynamic_slice_in_dim(delta, me_index * per, per, 0)
        coeffs = coeffs.at[local].add(own)
        change = jnp.dot(
            kernel(features, block_x),
            delta,
            precision=lax.Precision.HIGHEST,
            preferred_element_type=jnp.float32,
        )
        residual = residual - change
        residual = residual.at[local].add(-1.0 * own)
    return (coeffs, residual)


def solution(mesh):
    in_specs = (
        P(("groups", "wide"), None),
        P(("groups", "wide"), None),
        P("groups"),
        P(("groups", "wide")),
    )
    out_specs = (P(("groups", "wide"), None), P(("groups", "wide"), None))
    return jax.shard_map(body, mesh=mesh, in_specs=in_specs, out_specs=out_specs, check_vma=False)
```

profile of v0, /device:TPU:0, one launch (start us, length us, event | category | flops | bytes accessed | tf_op | source)
XLA Modules:
  0.0 971.5 jit_solution(15214842117377222493)
XLA Ops:
  10.4 24.6 %all-gather.2 = f32[1024,64]{1,0:T(8,128)S(1)} all-gather(f32[64,64]{1,0:T(8,128)S(1)} %gather_fusion.2), channel_id=4, replica_groups=mesh['groups'=2,'wide'=16] {'wide'}, dimensions={0}, use_global_device_ids=true | all-gather | bytes 278528 | tf_op jit(solution)/shard_map/all_gather | solution.py:57
  43.2 11.7 %cholesky.606 = f32[128,128]{1,0:T(8,128)S(1)} custom-call(f32[128,128]{1,0:T(8,128)S(1)} %cholesky.772), custom_call_target="Cholesky" | custom-call | tf_op jit(solution)/shard_map/jit(cholesky)/cholesky | solution.py:21
  65.6 11.9 %cholesky.625 = f32[128,128]{1,0:T(8,128)S(1)} custom-call(f32[128,128]{1,0:T(8,128)S(1)} %cholesky.776), custom_call_target="Cholesky" | custom-call | tf_op jit(solution)/shard_map/jit(cholesky)/cholesky | solution.py:21
  90.0 11.7 %cholesky.646 = f32[128,128]{1,0:T(8,128)S(1)} custom-call(f32[128,128]{1,0:T(8,128)S(1)} %cholesky.781), custom_call_target="Cholesky" | custom-call | tf_op jit(solution)/shard_map/jit(cholesky)/cholesky | solution.py:21
  112.9 13.2 %convolution_dynamic-update-slice_fusion.6 = f32[512,512]{1,0:T(8,128)S(1)} fusion(f32[512,512]{1,0:T(8,128)S(1)} %get-tuple-element.129, f32[256,128]{1,0:T(8,128)S(1)} %convolution_subtract_fusion.13, f32[1,128,128]{1,2,0:T(8,128)S(1)} %custom-call.52), kind=kOutput, calls=%fused_computation.74 | convolution fusion | flops 25165824 | bytes 196608 | tf_op jit(solution)/shard_map/jit(cholesky)/cholesky | solution.py:21
  126.5 11.7 %cholesky.663 = f32[128,128]{1,0:T(8,128)S(1)} custom-call(f32[128,128]{1,0:T(8,128)S(1)} %convolution_subtract_fusion.41), custom_call_target="Cholesky" | custom-call | tf_op jit(solution)/shard_map/jit(cholesky)/cholesky | solution.py:21
  140.8 11.6 %while.14 = (s32[]{:T(128)}, f32[512,512]{1,0:T(8,128)}, s32[4,2]{0,1:T(2,128)S(1)}, f32[4,128,128]{2,1,0:T(8,128)S(1)}, s32[]{:T(128)}) while((s32[]{:T(128)}, f32[512,512]{1,0:T(8,128)}, s32[4,2]{0,1:T(2,128)S(1)}, f32[4,128,128]{2,1,0:T(8,128)S(1)}, s32[]{:T(128)}) %tuple.158), condition=%wide.while_cond.clone, body=%wide.while_body.clone.sunk | while | flops 2 | bytes 131181 | solution.py:22
  152.4 39.3 %custom-call.53 = f32[4,128,128]{1,2,0:T(8,128)S(1)} custom-call(f32[4,128,128]{2,1,0:T(8,128)S(1)} %get-tuple-element.51), custom_call_target="InvertDiagBlocksLowerTriangular" | custom-call | tf_op jit(solution)/shard_map/triangular_solve/custom-call.3 | solution.py:22
  207.6 11.7 %cholesky.678 = f32[128,128]{1,0:T(8,128)S(1)} custom-call(f32[128,128]{1,0:T(8,128)S(1)} %cholesky.785), custom_call_target="Cholesky" | custom-call | tf_op jit(solution)/shard_map/jit(cholesky)/cholesky | solution.py:31
  236.6 11.7 %cholesky.697 = f32[128,128]{1,0:T(8,128)S(1)} custom-call(f32[128,128]{1,0:T(8,128)S(1)} %cholesky.789), custom_call_target="Cholesky" | custom-call | tf_op jit(solution)/shard_map/jit(cholesky)/cholesky | solution.py:31
  263.9 13.2 %cholesky.718 = f32[128,128]{1,0:T(8,128)} custom-call(f32[128,128]{1,0:T(8,128)} %cholesky.794), custom_call_target="Cholesky" | custom-call | tf_op jit(solution)/shard_map/jit(cholesky)/cholesky | solution.py:31
  293.5 11.7 %cholesky.735 = f32[128,128]{1,0:T(8,128)S(1)} custom-call(f32[128,128]{1,0:T(8,128)S(1)} %convolution_subtract_fusion.40), custom_call_target="Cholesky" | custom-call | tf_op jit(solution)/shard_map/jit(cholesky)/cholesky | solution.py:31
  311.5 23.2 %while.15 = (s32[]{:T(128)}, f32[1024,1024]{1,0:T(8,128)}, s32[8,2]{0,1:T(2,128)S(1)}, f32[8,128,128]{2,1,0:T(8,128)S(1)}, s32[]{:T(128)}) while((s32[]{:T(128)}, f32[1024,1024]{1,0:T(8,128)}, s32[8,2]{0,1:T(2,128)S(1)}, f32[8,128,128]{2,1,0:T(8,128)S(1)}, s32[]{:T(128)}) %tuple.161), condition=%wide.while_cond.2.clone, body=%wide.while_body.2.clone.sunk | while | flops 2 | bytes 131181 | solution.py:39
  334.7 79.2 %custom-call.58 = f32[8,128,128]{1,2,0:T(8,128)} custom-call(f32[8,128,128]{2,1,0:T(8,128)S(1)} %get-tuple-element.53), custom_call_target="InvertDiagBlocksLowerTriangular" | custom-call | tf_op jit(solution)/shard_map/triangular_solve/custom-call.9 | solution.py:39
  416.4 19.1 %all-gather = f32[1024,64]{1,0:T(8,128)S(1)} all-gather(f32[64,64]{1,0:T(8,128)S(1)} %gather_fusion), channel_id=2, replica_groups=mesh['groups'=2,'wide'=16] {'wide'}, dimensions={0}, use_global_device_ids=true | all-gather | bytes 278528 | tf_op jit(solution)/shard_map/all_gather | solution.py:57
  443.8 11.7 %cholesky.462 = f32[128,128]{1,0:T(8,128)S(1)} custom-call(f32[128,128]{1,0:T(8,128)S(1)} %cholesky.746), custom_call_target="Cholesky" | custom-call | tf_op jit(solution)/shard_map/jit(cholesky)/cholesky | solution.py:21
  466.2 12.1 %cholesky.481 = f32[128,128]{1,0:T(8,128)S(1)} custom-call(f32[128,128]{1,0:T(8,128)S(1)} %cholesky.750), custom_call_target="Cholesky" | custom-call | tf_op jit(solution)/shard_map/jit(cholesky)/cholesky | solution.py:21
  490.8 11.7 %cholesky.502 = f32[128,128]{1,0:T(8,128)S(1)} custom-call(f32[128,128]{1,0:T(8,128)S(1)} %cholesky.755), custom_call_target="Cholesky" | custom-call | tf_op jit(solution)/shard_map/jit(cholesky)/cholesky | solution.py:21
  514.4 11.7 %cholesky.519 = f32[128,128]{1,0:T(8,128)S(1)} custom-call(f32[128,128]{1,0:T(8,128)S(1)} %convolution_subtract_fusion.47), custom_call_target="Cholesky" | custom-call | tf_op jit(solution)/shard_map/jit(cholesky)/cholesky | solution.py:21
  536.4 39.3 %custom-call.44 = f32[4,128,128]{1,2,0:T(8,128)S(1)} custom-call(f32[4,128,128]{2,1,0:T(8,128)S(1)} %get-tuple-element.48), custom_call_target="InvertDiagBlocksLowerTriangular" | custom-call | tf_op jit(solution)/shard_map/triangular_solve/custom-call.3 | solution.py:22
  590.8 11.7 %cholesky.534 = f32[128,128]{1,0:T(8,128)S(1)} custom-call(f32[128,128]{1,0:T(8,128)S(1)} %cholesky.759), custom_call_target="Cholesky" | custom-call | tf_op jit(solution)/shard_map/jit(cholesky)/cholesky | solution.py:31
  615.8 11.7 %cholesky.553 = f32[128,128]{1,0:T(8,128)S(1)} custom-call(f32[128,128]{1,0:T(8,128)S(1)} %cholesky.763), custom_call_target="Cholesky" | custom-call | tf_op jit(solution)/shard_map/jit(cholesky)/cholesky | solution.py:31
  641.5 11.7 %cholesky.574 = f32[128,128]{1,0:T(8,128)S(1)} custom-call(f32[128,128]{1,0:T(8,128)S(1)} %cholesky.768), custom_call_target="Cholesky" | custom-call | tf_op jit(solution)/shard_map/jit(cholesky)/cholesky | solution.py:31
  665.9 11.7 %cholesky.591 = f32[128,128]{1,0:T(8,128)S(1)} custom-call(f32[128,128]{1,0:T(8,128)S(1)} %convolution_subtract_fusion.46), custom_call_target="Cholesky" | custom-call | tf_op jit(solution)/shard_map/jit(cholesky)/cholesky | solution.py:31
  685.1 23.2 %while.13 = (s32[]{:T(128)}, f32[1024,1024]{1,0:T(8,128)}, s32[8,2]{0,1:T(2,128)S(1)}, f32[8,128,128]{2,1,0:T(8,128)S(1)}, s32[]{:T(128)}) while((s32[]{:T(128)}, f32[1024,1024]{1,0:T(8,128)}, s32[8,2]{0,1:T(2,128)S(1)}, f32[8,128,128]{2,1,0:T(8,128)S(1)}, s32[]{:T(128)}) %tuple.165), condition=%wide.while_cond.2, body=%wide.while_body.2.sunk | while | flops 2 | bytes 131181 | solution.py:39
  708.3 78.6 %custom-call.49 = f32[8,128,128]{1,2,0:T(8,128)S(1)} custom-call(f32[8,128,128]{2,1,0:T(8,128)S(1)} %get-tuple-element.50), custom_call_target="InvertDiagBlocksLowerTriangular" | custom-call | tf_op jit(solution)/shard_map/triangular_solve/custom-call.9 | solution.py:39
  789.4 20.7 %all-gather.1 = f32[1024,128]{1,0:T(8,128)S(1)} all-gather(f32[64,128]{1,0:T(8,128)S(1)} %gather_fusion.1), channel_id=3, replica_groups=mesh['groups'=2,'wide'=16] {'wide'}, dimensions={0}, use_global_device_ids=true | all-gather | bytes 557056 | tf_op jit(solution)/shard_map/all_gather | solution.py:58
  825.2 20.9 %fusion.286 = f32[1024,6144]{0,1:T(8,128)S(1)} fusion(f32[1024,64]{1,0:T(8,128)S(1)} %all-gather, f32[6144,64]{0,1:T(8,128)S(1)} %copy-done), kind=kOutput, calls=%fused_computation.553 | convolution fusion | flops 4831838208 | bytes 27000832 | tf_op jit(solution)/shard_map/dot_general | solution.py:13
  846.3 26.0 %fusion.22 = f32[6144,128]{1,0:T(8,128)} fusion(f32[6144,128]{1,0:T(8,128)} %param.12, f32[1024,128]{1,0:T(8,128)S(1)} %constant_dynamic-update-slice_fusion.36, f32[1024,6144]{0,1:T(8,128)S(1)} %fusion.286, f32[1024]{0:T(1024)S(1)} %copy-done.16, f32[6144]{0:T(1024)S(1)} %multiply_reduce_fusion), kind=kOutput, calls=%fused_computation.38 | convolution fusion | flops 9695920128 | bytes 32010240 | tf_op jit(solution)/shard_map/dot_general | solution.py:65
  879.4 19.2 %all-gather.3 = f32[1024,128]{1,0:T(8,128)S(1)} all-gather(f32[64,128]{1,0:T(8,128)S(1)} %gather_fusion.3), channel_id=5, replica_groups=mesh['groups'=2,'wide'=16] {'wide'}, dimensions={0}, use_global_device_ids=true | all-gather | bytes 557056 | tf_op jit(solution)/shard_map/all_gather | solution.py:58
  913.6 20.9 %fusion.287 = f32[1024,6144]{0,1:T(8,128)S(1)} fusion(f32[1024,64]{1,0:T(8,128)S(1)} %all-gather.2, f32[6144,64]{0,1:T(8,128)S(1)} %copy-done), kind=kOutput, calls=%fused_computation.554 | convolution fusion | flops 4831838208 | bytes 27000832 | tf_op jit(solution)/shard_map/dot_general | solution.py:13
  934.5 24.6 %fusion.25 = f32[6144,128]{1,0:T(8,128)} fusion(f32[6144,128]{1,0:T(8,128)S(1)} %copy-done.12, f32[1024,128]{1,0:T(8,128)S(1)} %constant_dynamic-update-slice_fusion.79, f32[1024,6144]{0,1:T(8,128)S(1)} %fusion.287, f32[1024]{0:T(1024)S(1)} %copy-done.14, f32[6144]{0:T(1024)S(1)} %multiply_reduce_fusion), kind=kOutput, calls=%fused_computation.39 | convolution fusion | flops 9695920128 | bytes 32010240 | tf_op jit(solution)/shard_map/dot_general | solution.py:65
  (360 shorter events, 349.3 us)
Async XLA Ops:
  4.6 3.3 copy-start.17
  35.2 4.2 copy-start.13
  39.4 1.9 copy-start.3
  200.1 0.7 copy-start.8
  206.6 1.0 copy-start.6
  235.9 0.7 copy-start.10
  306.7 107.2 %copy-start.18 = (s32[64]{0:T(128)S(1)}, s32[64]{0:T(128)}, u32[]{:S(2)}) copy-start(s32[64]{0:T(128)} %get-tuple-element.173) | copy-start | bytes 772
  435.7 4.2 copy-start.15
  439.9 2.0 copy-start.4
  536.3 42.8 %copy-start.5 = (f32[512,512]{1,0:T(8,128)}, f32[512,512]{1,0:T(8,128)S(1)}, u32[]{:S(2)}) copy-start(f32[512,512]{1,0:T(8,128)S(1)} %get-tuple-element.391) | copy-start | bytes 3145732
  589.8 1.0 copy-start.7
  789.4 27.0 %copy-start.2 = (f32[1024,1024]{1,0:T(8,128)S(1)}, f32[1024,1024]{1,0:T(8,128)}, u32[]{:S(2)}) copy-start(f32[1024,1024]{1,0:T(8,128)} %get-tuple-element.389) | copy-start | bytes 12582916
  820.0 5.2 copy-start
  825.2 21.1 %copy-start.11 = (f32[1024,128]{1,0:T(8,128)}, f32[1024,128]{1,0:T(8,128)S(1)}, u32[]{:S(2)}) copy-start(f32[1024,128]{1,0:T(8,128)S(1)} %constant_dynamic-update-slice_fusion.36) | copy-start | bytes 1572868
  825.2 21.1 %copy-start.16 = (f32[1024]{0:T(1024)S(1)}, f32[1024]{0:T(1024)}, u32[]{:S(2)}) copy-start(f32[1024]{0:T(1024)} %copy-done.15) | copy-start | bytes 12292
  846.3 52.3 %copy-start.9 = (f32[8,128,128]{1,2,0:T(8,128)S(1)}, f32[8,128,128]{1,2,0:T(8,128)}, u32[]{:S(2)}) copy-start(f32[8,128,128]{1,2,0:T(8,128)} %custom-call.58) | copy-start | bytes 1572868
  879.4 25.5 %copy-start.1 = (f32[1024,1024]{1,0:T(8,128)S(1)}, f32[1024,1024]{1,0:T(8,128)}, u32[]{:S(2)}) copy-start(f32[1024,1024]{1,0:T(8,128)} %get-tuple-element.388) | copy-start | bytes 12582916
  913.6 20.9 %copy-start.12 = (f32[6144,128]{1,0:T(8,128)S(1)}, f32[6144,128]{1,0:T(8,128)}, u32[]{:S(2)}) copy-start(f32[6144,128]{1,0:T(8,128)} %scatter_custom_fusion.1) | copy-start | bytes 9437188
  913.6 20.9 %copy-start.14 = (f32[1024]{0:T(1024)S(1)}, f32[1024]{0:T(1024)}, u32[]{:S(2)}) copy-start(f32[1024]{0:T(1024)} %copy-done.13) | copy-start | bytes 12292
where the time goes:
time: 983 us; the launch traced here: 971 us
  other arithmetic  595 us (61%)
  matrix products  183 us (19%)
  local copies, waits for them, and re-layouts  95 us (10%)
  blocking collectives  83.6 us (9%)
  between operations  14.3 us (1%)
    another operation x5, other arithmetic, solve_with(): lax.linalg.triangular_solve(factor, halfway, left_side=True, lower=True,...  168 us
    another operation x30, other arithmetic, factorize(): bottom = jnp.linalg.cholesky(schur)  164 us
    another operation x28, other arithmetic, factorize(): top = jnp.linalg.cholesky(gram[:half, :half])  157 us
    another operation x5, other arithmetic, factorize(): lax.linalg.triangular_solve(top, gram[half:, :half], left_side=False, low...  81.1 us
    dot_general x2, matrix products, body(): jnp.dot(kernel(features, block_x), delta, precision=lax.Precision.HIGHEST...  50.6 us
    dot_general x4, matrix products, kernel(): jnp.dot(left, right.T, precision=lax.Precision.HIGHEST, preferred_element...  50.2 us
    another operation x59, local copies, waits for them, and re-layouts, solve_with(): lax.linalg.triangular_solve(factor, halfway, left_side=True, lower=True,...  46.2 us
    all_gather x2, blocking collectives, body(): lax.all_gather(features[local], 'wide', axis=0, tiled=True)  43.7 us

commit v1 on v0

v1 whole, which is shorter than its diff:
```python
import functools
import math

import jax
import jax.numpy as jnp
from jax import lax
from jax.experimental import pallas as pl
from jax.experimental.pallas import tpu as pltpu
from jax.sharding import PartitionSpec as P

BLOCK = 1024
STEPS = 2
TILE = 256
SQUARINGS = 6
LOG2E = math.log2(math.e)
F32 = jnp.float32
BF16 = jnp.bfloat16
HIGHEST = lax.Precision.HIGHEST
NT = (((1,), (1,)), ((), ()))
NN = (((1,), (0,)), ((), ()))
TN = (((0,), (0,)), ((), ()))


def full(a, b, dims=NN):
    return lax.dot_general(a, b, dims, precision=HIGHEST, preferred_element_type=F32)


def split2(a):
    high = a.astype(BF16)
    return high, (a - high.astype(F32)).astype(BF16)


def three(a, b, dims=NN):
    dot = functools.partial(lax.dot_general, dimension_numbers=dims, preferred_element_type=F32)
    return dot(a[0], b[0]) + (dot(a[0], b[1]) + dot(a[1], b[0]))


def parts3(x):
    xx = jnp.concatenate([x, x], axis=1)
    high = xx.astype(BF16).astype(F32)
    rest = xx - high
    mid = rest.astype(BF16).astype(F32)
    low = rest - mid
    first = lax.broadcasted_iota(jnp.int32, xx.shape, 1) < x.shape[1]
    return high, mid, low, first


def pack_left(x):
    high, mid, low, first = parts3(x)
    return jnp.concatenate(
        [high.astype(BF16), mid.astype(BF16), jnp.where(first, high, low).astype(BF16)], axis=1
    )


def pack_right(x):
    high, mid, low, first = parts3(x)
    both = jnp.where(first, high, mid).astype(BF16)
    return jnp.concatenate([both, both, jnp.where(first, low, high).astype(BF16)], axis=1)


def left_side(x):
    return pack_left(x * (LOG2E / 16.0)), jnp.sum(x * x, axis=1, keepdims=True) * (LOG2E / 32.0)


def gauss(left, left_sq, right, right_sq):
    cross = lax.dot_general(left, right, NT, preferred_element_type=F32)
    return jnp.exp2(cross - left_sq - right_sq)


def bounds_radius():
    low, high = 0.99, TILE + 2.0
    return 2.0 / (low + high), (high - low) / (high + low)


def solve(same, gathered, right, right_sq, gram, weights, inverse, power, rhs, delta):
    shards, rows2, _ = gathered.shape
    per = rows2 // STEPS
    tiles = BLOCK // TILE
    chunk = TILE // per

    def rows_of(system, tile, lanes):
        part = gathered[pl.ds(tile * chunk, chunk), pl.ds(system * per, per), lanes]
        return part.reshape(TILE, part.shape[-1])

    feats = slice(128, 192)
    ones = jnp.ones((8, 64), F32)
    for system in range(STEPS):
        for tile in range(tiles):
            x = rows_of(system, tile, feats)
            at = pl.ds(system * BLOCK + tile * TILE, TILE)
            right[at, :] = pack_right(x)
            right_sq[:, at] = full(ones, x * x, NT) * (LOG2E / 32.0)
            rhs[at, :] = rows_of(system, tile, slice(0, 128))
    eye = (
        lax.broadcasted_iota(jnp.int32, (TILE, TILE), 0)
        == lax.broadcasted_iota(jnp.int32, (TILE, TILE), 1)
    ).astype(F32)
    for system in range(STEPS):
        for tile in range(tiles):
            left, left_sq = left_side(rows_of(system, tile, feats))
            for other in range(tile + 1):
                at = pl.ds(system * BLOCK + other * TILE, TILE)
                value = gauss(left, left_sq, right[at, :], right_sq[0:1, at])
                if other == tile:
                    value = value + 1.0 * eye
                gram[system, tile * TILE : (tile + 1) * TILE, other * TILE : (other + 1) * TILE] = value

    def span(first, last=None):
        return slice(first * TILE, (first + 1 if last is None else last) * TILE)

    def forward(system, k):
        z = rhs[system * BLOCK + k * TILE : system * BLOCK + (k + 1) * TILE, :]
        if k + 1 < tiles:
            at = slice(system * BLOCK + (k + 1) * TILE, (system + 1) * BLOCK)
            rhs[at, :] = rhs[at, :] - full(weights[system, span(k + 1, tiles), span(k)], z)

    def backward(system, k):
        at = slice(system * BLOCK + k * TILE, system * BLOCK + (k + 1) * TILE)
        value = full(inverse[system, k], rhs[at, :])
        if k + 1 < tiles:
            below = delta[system * BLOCK + (k + 1) * TILE : (system + 1) * BLOCK, :]
            value = value - full(weights[system, span(k + 1, tiles), span(k)], below, TN)
        delta[at, :] = value

    for k in range(tiles):
        scale, radius = bounds_radius()
        for system in range(STEPS):
            power[system] = eye - scale * gram[system, span(k), span(k)]
            inverse[system, k] = scale * eye

        def squaring(_, rho):
            square = rho * rho
            step = 2.0 / (2.0 - square)
            for system in range(STEPS):
                e = split2(power[system])
                x = inverse[system, k]
                x_new = step * (x + three(split2(x), e))
                e_new = (1.0 - step) * eye + step * three(e, e)
                inverse[system, k] = x_new
                power[system] = e_new
            return square / (2.0 - square)

        lax.fori_loop(0, SQUARINGS, squaring, jnp.float32(radius))
        for system in range(STEPS):
            x = inverse[system, k]
            error = eye - full(gram[system, span(k), span(k)], x)
            inverse[system, k] = x + three(split2(x), split2(error))
        for system in range(STEPS):
            if k + 1 < tiles:
                below = gram[system, span(k + 1, tiles), span(k)]
                weights[system, span(k + 1, tiles), span(k)] = full(below, inverse[system, k])
        for system in range(STEPS):
            for j in range(k + 1, tiles):
                at = (system, span(j, tiles), span(j))
                gram[at] = gram[at] - full(
                    weights[system, span(j, tiles), span(k)], gram[system, span(j), span(k)], NT
                )
        forward(0, k)
    for k in reversed(range(tiles)):
        backward(0, k)
    delta_one = split2(delta[0:BLOCK, :])
    for tile in range(tiles):
        left, left_sq = left_side(rows_of(1, tile, feats))
        at = slice(BLOCK + tile * TILE, BLOCK + (tile + 1) * TILE)
        cross = gauss(left, left_sq, right[0:BLOCK, :], right_sq[0:1, 0:BLOCK])
        change = three(split2(cross), delta_one) + same * delta[tile * TILE : (tile + 1) * TILE, :]
        rhs[at, :] = rhs[at, :] - change
    for k in range(tiles):
        forward(1, k)
    for k in reversed(range(tiles)):
        backward(1, k)


def kernel(
    scalars, gathered, features, targets, coeffs, residual,
    right, right_sq, gram, weights, inverse, power, rhs, delta, packed,
):
    per = gathered.shape[1] // STEPS
    rows = features.shape[0]
    here = pl.program_id(0)

    @pl.when(here == 0)
    def _():
        me = scalars[STEPS * per]
        same = scalars[STEPS * per + 1].astype(F32)
        solve(same, gathered, right, right_sq, gram, weights, inverse, power, rhs, delta)
        high, low = split2(delta[...])
        packed[...] = jnp.concatenate([high, low], axis=1)
        coeffs[...] = jnp.zeros_like(coeffs)
        for step in range(STEPS):

            def put(j, _):
                row = scalars[step * per + j]
                own = delta[pl.ds(step * BLOCK + me * per + j, 1), :]
                coeffs[pl.ds(row, 1), :] = coeffs[pl.ds(row, 1), :] + own
                return 0

            lax.fori_loop(0, per, put, 0)

    left, left_sq = left_side(features[...])
    width = 512
    total = jnp.zeros((rows, 128), F32)
    for at in range(0, STEPS * BLOCK, width):
        cols = slice(at, at + width)
        value = gauss(left, left_sq, right[cols, :], right_sq[0:1, cols])
        high, low = split2(value)
        wide = jnp.dot(high, packed[cols, :], preferred_element_type=F32)
        narrow = jnp.dot(low, packed[cols, 0:128], preferred_element_type=F32)
        total = total + (wide[:, 0:128] + (wide[:, 128:256] + narrow))
    mine = coeffs[pl.ds(pl.multiple_of(here * rows, rows), rows), :]
    residual[...] = targets[...] - total - mine


def body(features, targets, block_ids, order):
    shards = lax.axis_size("wide")
    me = lax.axis_index("wide").astype(jnp.int32)
    per = BLOCK // shards
    rows_dev, feat = features.shape
    out = targets.shape[1]
    local = jnp.concatenate(
        [lax.dynamic_slice_in_dim(order, block_ids[step] * per, per, 0) for step in range(STEPS)]
    )
    rows = jnp.concatenate([targets[local], features[local]], axis=1)
    gathered = lax.all_gather(rows, "wide", axis=0)
    same = (block_ids[0] == block_ids[1]).astype(jnp.int32)
    scalars = jnp.concatenate([local, jnp.stack([me, same])])
    tile = 512
    grid_spec = pltpu.PrefetchScalarGridSpec(
        num_scalar_prefetch=1,
        grid=(rows_dev // tile,),
        in_specs=[
            pl.BlockSpec((shards, STEPS * per, out + feat), lambda i, s: (0, 0, 0)),
            pl.BlockSpec((tile, feat), lambda i, s: (i, 0)),
            pl.BlockSpec((tile, out), lambda i, s: (i, 0)),
        ],
        out_specs=[
            pl.BlockSpec((rows_dev, out), lambda i, s: (0, 0)),
            pl.BlockSpec((tile, out), lambda i, s: (i, 0)),
        ],
        scratch_shapes=[
            pltpu.VMEM((STEPS * BLOCK, 6 * feat), BF16),
            pltpu.VMEM((8, STEPS * BLOCK), F32),
            pltpu.VMEM((STEPS, BLOCK, BLOCK), F32),
            pltpu.VMEM((STEPS, BLOCK, BLOCK), F32),
            pltpu.VMEM((STEPS, BLOCK // TILE, TILE, TILE), F32),
            pltpu.VMEM((STEPS, TILE, TILE), F32),
            pltpu.VMEM((STEPS * BLOCK, out), F32),
            pltpu.VMEM((STEPS * BLOCK, out), F32),
            pltpu.VMEM((STEPS * BLOCK, 2 * out), BF16),
        ],
    )
    return pl.pallas_call(
        kernel,
        grid_spec=grid_spec,
        out_shape=[jax.ShapeDtypeStruct((rows_dev, out), F32)] * 2,
        compiler_params=pltpu.CompilerParams(
            dimension_semantics=("arbitrary",), vmem_limit_bytes=56 * 1024 * 1024
        ),
        cost_estimate=pl.CostEstimate(
            flops=2 * rows_dev * STEPS * BLOCK * (feat + out) + 2 * STEPS * BLOCK**3,
            bytes_accessed=4 * rows_dev * (feat + 3 * out),
            transcendentals=rows_dev * STEPS * BLOCK,
        ),
        name="block_solve_and_update",
    )(scalars, gathered, features, targets)


def solution(mesh):
    in_specs = (
        P(("groups", "wide"), None),
        P(("groups", "wide"), None),
        P("groups"),
        P(("groups", "wide")),
    )
    out_specs = (P(("groups", "wide"), None), P(("groups", "wide"), None))
    return jax.shard_map(body, mesh=mesh, in_specs=in_specs, out_specs=out_specs, check_vma=False)
```

time: 983 us -> 148 us (0.15); the launches traced: 971 us -> 148 us
  other arithmetic: 595 us -> 1.42 us
  matrix products: 183 us -> 0 us
  local copies, waits for them, and re-layouts: 95 us -> 8.57 us
  blocking collectives: 83.6 us -> 0 us
  Pallas kernels: 0 us -> 79.1 us
  waiting for transfers between devices: 0 us -> 42.4 us
    another operation x68 -> x0, other arithmetic: 571 us -> none  [the longest x5 168 us: solve_with(): lax.linalg.triangular_solve(factor, halfway, left_side=True, lower=True,...]
    dot_general x8 -> x0, matrix products: 107 us -> none  [the longest x2 50.6 us: body(): jnp.dot(kernel(features, block_x), delta, precision=lax.Precision.HIGHEST...]
    all_gather x4 -> x0, blocking collectives: 83.6 us -> none  [the longest x2 43.7 us: body(): lax.all_gather(features[local], 'wide', axis=0, tiled=True)]
    pallas_call x0 -> x1, Pallas kernels: none -> 79.1 us  [body(): pl.pallas_call(kernel, grid_spec=grid_spec, out_shape=[jax.ShapeDtypeStru...]
    another operation x98 -> x0, matrix products: 76.2 us -> none  [the longest x30 17.3 us: solve_with(): lax.linalg.triangular_solve(factor, right_side, left_side=True, lower=True)]
    another operation x108 -> x0, local copies, waits for them, and re-layouts: 69.6 us -> none  [the longest x59 46.2 us: solve_with(): lax.linalg.triangular_solve(factor, halfway, left_side=True, lower=True,...]
    all_gather x0 -> x1, waiting for transfers between devices: none -> 42.4 us  [body(): gathered = lax.all_gather(rows, 'wide', axis=0)]
    scatter-add x4 -> x0, other arithmetic: 16.5 us -> none  [the longest x2 9.14 us: body(): residual = residual.at[local].add(-1.0 * own)]
  transfers between devices with their start and end apart: 0 -> 1, of which waited for: 0 -> 1; matrix products, arithmetic and copies ran while one was open for 0% -> 0% of each run, Pallas kernels for 0% -> 0%
where the time goes in v1:
time: 148 us
  Pallas kernels  79.1 us (53%)
  waiting for transfers between devices  42.4 us (29%)
  between operations  16.5 us (11%)
  local copies, waits for them, and re-layouts  8.57 us (6%)
    pallas_call x1, Pallas kernels, body(): pl.pallas_call(kernel, grid_spec=grid_spec, out_shape=[jax.ShapeDtypeStru...  79.1 us
    all_gather x1, waiting for transfers between devices, body(): gathered = lax.all_gather(rows, 'wide', axis=0)  42.4 us
    gather x2, local copies, waits for them, and re-layouts, body(): rows = jnp.concatenate([targets[local], features[local]], axis=1)  4.32 us
  transfers between devices with their start and end apart: 1, of which 1 were waited for; matrix products, arithmetic and copies ran while one was open for 0% of the time, Pallas kernels for 0%

profile of v1, /device:TPU:0, one launch (start us, length us, event | category | flops | bytes accessed | tf_op | source)
XLA Modules:
  0.0 148.0 jit_solution(8040153774647664613)
XLA Ops:
  7.2 0.0 all-gather.3.cloned.1.call-start
  7.2 1.3 fusion.2
  9.8 0.8 fusion.1
  10.6 0.1 fusion
  10.7 2.1 %copy.6.features = f32[6144,64]{1,0:T(8,128)S(1)} copy(f32[6144,64]{0,1:T(8,128)} %param.4) | data formatting | bytes 3145728 | tf_op args[0]
  12.8 0.0 copy-start
  12.8 3.7 %gather_fusion = f32[128,128]{1,0:T(8,128)S(1)} fusion(f32[6144,128]{1,0:T(8,128)} %targets.1, s32[1024]{0:T(1024)S(1)} %pad_clamp_fusion), kind=kCustom, calls=%fused_computation | custom fusion | bytes 131584 | tf_op jit(solution)/shard_map/gather | solution.py:223
  16.5 0.6 gather_fusion.1
  17.1 0.7 pad_maximum_fusion
  17.8 0.0 all-gather.3.cloned.1.call-update
  19.0 0.7 pad_add_fusion.scalars
  19.7 42.4 %all-gather.3.cloned.1.call-done = f32[2048,192]{1,0:T(8,128)} async-done(((f32[128,192]{1,0:T(8,128)}), f32[2048,192]{1,0:T(8,128)}) %all-gather.3.cloned.1.call-update) | async-done | bytes 1572880 | tf_op jit(solution)/shard_map/all_gather | solution.py:224
  62.1 0.0 copy-done
  62.1 79.1 %block_solve_and_update.1 = (f32[6144,128]{1,0:T(8,128)}, f32[6144,128]{1,0:T(8,128)}) custom-call(s32[130]{0:T(256)} %pad_add_fusion.scalars, f32[16,128,192]{2,1,0:T(8,128)} %bitcast.10, f32[6144,64]{1,0:T(8,128)} %copy-done, f32[6144,128]{1,0:T(8,128)} %targets.1), custom_call_target="tpu_custom_call" | custom-call | flops 9126805504 | bytes 11010048 | tf_op jit(solution)/shard_map/block_solve_and_update/pallas_call | solution.py:252
  (1 shorter events, 0.0 us)
Async XLA Ops:
  7.2 54.9 %all-gather.3.cloned.1.call-start = ((), (), s32[]{:S(2)}) async-start(), calls=%async_computation | async-start | bytes 2228224 | tf_op jit(solution)/shard_map/all_gather | solution.py:224
  12.8 49.3 %copy-start = (f32[6144,64]{1,0:T(8,128)}, f32[6144,64]{1,0:T(8,128)S(1)}, u32[]{:S(2)}) copy-start(f32[6144,64]{1,0:T(8,128)S(1)} %copy.6.features) | copy-start | bytes 4718596
Sparse Core Ops, SparseCore 0:
  17.9 44.0 all-gather.2

commit v2 on v1

--- a/solution.py
+++ b/solution.py
@@ -72,55 +72,106 @@
     return 2.0 / (low + high), (high - low) / (high + low)
 
 
-def solve(same, gathered, right, right_sq, gram, weights, inverse, power, rhs, delta):
-    shards, rows2, _ = gathered.shape
-    per = rows2 // STEPS
+def tile_of(shared, tile, lanes):
+    chunk = TILE // shared.shape[1]
+    part = shared[tile * chunk : (tile + 1) * chunk, :, lanes]
+    return part.reshape(TILE, part.shape[-1])
+
+
+def feats_of(shared, system, tile):
+    half = shared.shape[2] // STEPS
+    return tile_of(shared, tile, slice(system * half, (system + 1) * half))
+
+
+def span(first, last=None):
+    return slice(first * TILE, (first + 1 if last is None else last) * TILE)
+
+
+def share(shards, x_ref, out_ref, send_near, recv_near, send_far, recv_far, own_sem):
+    me = lax.axis_index("wide")
+    other = me + 1 - 2 * lax.rem(me, 2)
+    half = shards // 2
+    barrier = pltpu.get_barrier_semaphore()
+    for d in range(1, half):
+        pl.semaphore_signal(
+            barrier, inc=1, device_id={"wide": lax.rem(me + 2 * d, shards)},
+            device_id_type=pl.DeviceIdType.MESH,
+        )
+    pl.semaphore_signal(
+        barrier, inc=1, device_id={"wide": other}, device_id_type=pl.DeviceIdType.MESH
+    )
+    pl.semaphore_wait(barrier, half)
+
+    own = pltpu.make_async_copy(x_ref, out_ref.at[me], own_sem)
+    own.start()
+    far = []
+    for d in range(1, half):
+        copy = pltpu.make_async_remote_copy(
+            src_ref=x_ref, dst_ref=out_ref.at[me],
+            send_sem=send_far.at[d], recv_sem=recv_far.at[d],
+            device_id={"wide": lax.rem(me + 2 * d, shards)},
+            device_id_type=pl.DeviceIdType.MESH,
+        )
+        copy.start()
+        far.append(copy)
+
+    def to_other(d, src_ref, slot):
+        copy = pltpu.make_async_remote_copy(
+            src_ref=src_ref, dst_ref=out_ref.at[slot],
+            send_sem=send_near.at[d], recv_sem=recv_near.at[d],
+            device_id={"wide": other}, device_id_type=pl.DeviceIdType.MESH,
+        )
+        copy.start()
+        return copy
+
+    near = [to_other(0, x_ref, me)]
+    for d in range(1, half):
+        far[d - 1].wait_recv()
+        slot = lax.rem(me - 2 * d + shards, shards)
+        near.append(to_other(d, out_ref.at[slot], slot))
+    for copy in far:
+        copy.wait_send()
+    for copy in near:
+        copy.wait()
+    own.wait()
+
+
+def gather_rows(x):
+    shards = lax.axis_size("wide")
+    half = shards // 2
+    return pl.pallas_call(
+        functools.partial(share, shards),
+        out_shape=jax.ShapeDtypeStruct((shards,) + x.shape, x.dtype),
+        in_specs=[pl.BlockSpec(memory_space=pltpu.VMEM)],
+        out_specs=pl.BlockSpec(memory_space=pltpu.VMEM),
+        scratch_shapes=[pltpu.SemaphoreType.DMA((half,))] * 4 + [pltpu.SemaphoreType.DMA],
+        compiler_params=pltpu.CompilerParams(collective_id=0, has_side_effects=True),
+        name="share_rows",
+    )(x)
+
+
+def factor(shared, right, right_sq, weights, inverse, gram, power):
     tiles = BLOCK // TILE
-    chunk = TILE // per
-
-    def rows_of(system, tile, lanes):
-        part = gathered[pl.ds(tile * chunk, chunk), pl.ds(system * per, per), lanes]
-        return part.reshape(TILE, part.shape[-1])
-
-    feats = slice(128, 192)
-    ones = jnp.ones((8, 64), F32)
+    ones = jnp.ones((8, shared.shape[2] // STEPS), F32)
     for system in range(STEPS):
         for tile in range(tiles):
-            x = rows_of(system, tile, feats)
-            at = pl.ds(system * BLOCK + tile * TILE, TILE)
+            x = feats_of(shared, system, tile)
+            at = slice(system * BLOCK + tile * TILE, system * BLOCK + (tile + 1) * TILE)
             right[at, :] = pack_right(x)
             right_sq[:, at] = full(ones, x * x, NT) * (LOG2E / 32.0)
-            rhs[at, :] = rows_of(system, tile, slice(0, 128))
     eye = (
         lax.broadcasted_iota(jnp.int32, (TILE, TILE), 0)
         == lax.broadcasted_iota(jnp.int32, (TILE, TILE), 1)
     ).astype(F32)
     for system in range(STEPS):
         for tile in range(tiles):
-            left, left_sq = left_side(rows_of(system, tile, feats))
+            left, left_sq = left_side(feats_of(shared, system, tile))
             for other in range(tile + 1):
-                at = pl.ds(system * BLOCK + other * TILE, TILE)
+                at = slice(system * BLOCK + other * TILE, system * BLOCK + (other + 1) * TILE)
                 value = gauss(left, left_sq, right[at, :], right_sq[0:1, at])
                 if other == tile:
                     value = value + 1.0 * eye
-                gram[system, tile * TILE : (tile + 1) * TILE, other * TILE : (other + 1) * TILE] = value
-
-    def span(first, last=None):
-        return slice(first * TILE, (first + 1 if last is None else last) * TILE)
-
-    def forward(system, k):
-        z = rhs[system * BLOCK + k * TILE : system * BLOCK + (k + 1) * TILE, :]
-        if k + 1 < tiles:
-            at = slice(system * BLOCK + (k + 1) * TILE, (system + 1) * BLOCK)
-            rhs[at, :] = rhs[at, :] - full(weights[system, span(k + 1, tiles), span(k)], z)
-
-    def backward(system, k):
-        at = slice(system * BLOCK + k * TILE, system * BLOCK + (k + 1) * TILE)
-        value = full(inverse[system, k], rhs[at, :])
-        if k + 1 < tiles:
-            below = delta[system * BLOCK + (k + 1) * TILE : (system + 1) * BLOCK, :]
-            value = value - full(weights[system, span(k + 1, tiles), span(k)], below, TN)
-        delta[at, :] = value
+                gram[system, span(tile), span(other)] = value
 
     for k in range(tiles):
         scale, radius = bounds_radius()
@@ -145,22 +196,51 @@
             x = inverse[system, k]
             error = eye - full(gram[system, span(k), span(k)], x)
             inverse[system, k] = x + three(split2(x), split2(error))
+        if k + 1 == tiles:
+            break
         for system in range(STEPS):
-            if k + 1 < tiles:
-                below = gram[system, span(k + 1, tiles), span(k)]
-                weights[system, span(k + 1, tiles), span(k)] = full(below, inverse[system, k])
+            below = gram[system, span(k + 1, tiles), span(k)]
+            weights[system, span(k, tiles - 1), span(k)] = full(below, inverse[system, k])
         for system in range(STEPS):
             for j in range(k + 1, tiles):
                 at = (system, span(j, tiles), span(j))
                 gram[at] = gram[at] - full(
-                    weights[system, span(j, tiles), span(k)], gram[system, span(j), span(k)], NT
+                    weights[system, span(j - 1, tiles - 1), span(k)],
+                    gram[system, span(j), span(k)], NT,
                 )
+
+
+def solve(same, shared, wanted, right, right_sq, weights, inverse, rhs, delta):
+    tiles = BLOCK // TILE
+    per = shared.shape[1]
+    chunk = TILE // per
+    for system in range(STEPS):
+        for tile in range(tiles):
+            part = wanted[tile * chunk : (tile + 1) * chunk, system * per : (system + 1) * per, :]
+            at = slice(system * BLOCK + tile * TILE, system * BLOCK + (tile + 1) * TILE)
+            rhs[at, :] = part.reshape(TILE, part.shape[-1])
+
+    def forward(system, k):
+        if k + 1 < tiles:
+            z = rhs[system * BLOCK + k * TILE : system * BLOCK + (k + 1) * TILE, :]
+            at = slice(system * BLOCK + (k + 1) * TILE, (system + 1) * BLOCK)
+            rhs[at, :] = rhs[at, :] - full(weights[system, span(k, tiles - 1), span(k)], z)
+
+    def backward(system, k):
+        at = slice(system * BLOCK + k * TILE, system * BLOCK + (k + 1) * TILE)
+        value = full(inverse[system, k], rhs[at, :])
+        if k + 1 < tiles:
+            below = delta[system * BLOCK + (k + 1) * TILE : (system + 1) * BLOCK, :]
+            value = value - full(weights[system, span(k, tiles - 1), span(k)], below, TN)
+        delta[at, :] = value
+
+    for k in range(tiles):
         forward(0, k)
     for k in reversed(range(tiles)):
         backward(0, k)
     delta_one = split2(delta[0:BLOCK, :])
     for tile in range(tiles):
-        left, left_sq = left_side(rows_of(1, tile, feats))
+        left, left_sq = left_side(feats_of(shared, 1, tile))
         at = slice(BLOCK + tile * TILE, BLOCK + (tile + 1) * TILE)
         cross = gauss(left, left_sq, right[0:BLOCK, :], right_sq[0:1, 0:BLOCK])
         change = three(split2(cross), delta_one) + same * delta[tile * TILE : (tile + 1) * TILE, :]
@@ -171,11 +251,11 @@
         backward(1, k)
 
 
-def kernel(
-    scalars, gathered, features, targets, coeffs, residual,
-    right, right_sq, gram, weights, inverse, power, rhs, delta, packed,
+def update(
+    scalars, shared, wanted, right, right_sq, weights, inverse, features, targets,
+    coeffs, residual, rhs, delta, packed,
 ):
-    per = gathered.shape[1] // STEPS
+    per = shared.shape[1]
     rows = features.shape[0]
     here = pl.program_id(0)
 
@@ -183,7 +263,7 @@
     def _():
         me = scalars[STEPS * per]
         same = scalars[STEPS * per + 1].astype(F32)
-        solve(same, gathered, right, right_sq, gram, weights, inverse, power, rhs, delta)
+        solve(same, shared, wanted, right, right_sq, weights, inverse, rhs, delta)
         high, low = split2(delta[...])
         packed[...] = jnp.concatenate([high, low], axis=1)
         coeffs[...] = jnp.zeros_like(coeffs)
@@ -217,19 +297,45 @@
     per = BLOCK // shards
     rows_dev, feat = features.shape
     out = targets.shape[1]
+    tiles = BLOCK // TILE
     local = jnp.concatenate(
         [lax.dynamic_slice_in_dim(order, block_ids[step] * per, per, 0) for step in range(STEPS)]
     )
-    rows = jnp.concatenate([targets[local], features[local]], axis=1)
-    gathered = lax.all_gather(rows, "wide", axis=0)
+    wanted = lax.all_gather(targets[local], "wide", axis=0)
+    picked = features[local].reshape(STEPS, per, feat)
+    shared = gather_rows(jnp.concatenate([picked[0], picked[1]], axis=1))
     same = (block_ids[0] == block_ids[1]).astype(jnp.int32)
     scalars = jnp.concatenate([local, jnp.stack([me, same])])
+    limit = pltpu.CompilerParams(vmem_limit_bytes=56 * 1024 * 1024)
+    right, right_sq, weights, inverse = pl.pallas_call(
+        factor,
+        out_shape=[
+            jax.ShapeDtypeStruct((STEPS * BLOCK, 6 * feat), BF16),
+            jax.ShapeDtypeStruct((8, STEPS * BLOCK), F32),
+            jax.ShapeDtypeStruct((STEPS, BLOCK - TILE, BLOCK - TILE), F32),
+            jax.ShapeDtypeStruct((STEPS, tiles, TILE, TILE), F32),
+        ],
+        scratch_shapes=[
+            pltpu.VMEM((STEPS, BLOCK, BLOCK), F32),
+            pltpu.VMEM((STEPS, TILE, TILE), F32),
+        ],
+        compiler_params=limit,
+        cost_estimate=pl.CostEstimate(
+            flops=24 * STEPS * BLOCK**3, bytes_accessed=16 * BLOCK * BLOCK, transcendentals=0
+        ),
+        name="factor_blocks",
+    )(shared)
     tile = 512
+
+    def whole(array):
+        return pl.BlockSpec(array.shape, lambda i, s: (0,) * array.ndim)
+
+    fixed = (shared, wanted, right, right_sq, weights, inverse)
     grid_spec = pltpu.PrefetchScalarGridSpec(
         num_scalar_prefetch=1,
         grid=(rows_dev // tile,),
-        in_specs=[
-            pl.BlockSpec((shards, STEPS * per, out + feat), lambda i, s: (0, 0, 0)),
+        in_specs=[whole(array) for array in fixed]
+        + [
             pl.BlockSpec((tile, feat), lambda i, s: (i, 0)),
             pl.BlockSpec((tile, out), lambda i, s: (i, 0)),
         ],
@@ -238,31 +344,23 @@
             pl.BlockSpec((tile, out), lambda i, s: (i, 0)),
         ],
         scratch_shapes=[
-            pltpu.VMEM((STEPS * BLOCK, 6 * feat), BF16),
-            pltpu.VMEM((8, STEPS * BLOCK), F32),
-            pltpu.VMEM((STEPS, BLOCK, BLOCK), F32),
-            pltpu.VMEM((STEPS, BLOCK, BLOCK), F32),
-            pltpu.VMEM((STEPS, BLOCK // TILE, TILE, TILE), F32),
-            pltpu.VMEM((STEPS, TILE, TILE), F32),
             pltpu.VMEM((STEPS * BLOCK, out), F32),
             pltpu.VMEM((STEPS * BLOCK, out), F32),
             pltpu.VMEM((STEPS * BLOCK, 2 * out), BF16),
         ],
     )
     return pl.pallas_call(
-        kernel,
+        update,
         grid_spec=grid_spec,
         out_shape=[jax.ShapeDtypeStruct((rows_dev, out), F32)] * 2,
-        compiler_params=pltpu.CompilerParams(
-            dimension_semantics=("arbitrary",), vmem_limit_bytes=56 * 1024 * 1024
-        ),
+        compiler_params=limit,
         cost_estimate=pl.CostEstimate(
-            flops=2 * rows_dev * STEPS * BLOCK * (feat + out) + 2 * STEPS * BLOCK**3,
+            flops=2 * rows_dev * STEPS * BLOCK * (feat + out),
             bytes_accessed=4 * rows_dev * (feat + 3 * out),
             transcendentals=rows_dev * STEPS * BLOCK,
         ),
-        name="block_solve_and_update",
-    )(scalars, gathered, features, targets)
+        name="solve_and_update",
+    )(scalars, *fixed, features, targets)
 
 
 def solution(mesh):

time: 148 us -> 127 us (0.86)
  waiting for transfers between devices: 42.4 us -> 0.02 us
  Pallas kernels: 79.1 us -> 100 us
    all_gather x1, waiting for transfers between devices: 42.4 us -> 0.01 us  [body(): wanted = lax.all_gather(targets[local], 'wide', axis=0)]
    pallas_call x1 -> x3, Pallas kernels: 79.1 us -> 100 us  [the longest x1 52.7 us: body(): pl.pallas_call(update, grid_spec=grid_spec, out_shape=[jax.ShapeDtypeStru...]
  transfers between devices with their start and end apart: 1 -> 1, of which waited for: 1 -> 0; matrix products, arithmetic and copies ran while one was open for 0% -> 3% of each run, Pallas kernels for 0% -> 38%
where the time goes in v2:
time: 127 us; the launch traced here: 126 us
  Pallas kernels  100 us (79%)
  between operations  16.5 us (13%)
  local copies, waits for them, and re-layouts  8.01 us (6%)
  other arithmetic  1.68 us (1%)
    pallas_call x1, Pallas kernels, body(): pl.pallas_call(update, grid_spec=grid_spec, out_shape=[jax.ShapeDtypeStru...  52.7 us
    pallas_call x1, Pallas kernels, body(): pl.pallas_call(factor, out_shape=[jax.ShapeDtypeStruct((STEPS * BLOCK, 6...  33.5 us
    pallas_call x1, Pallas kernels, gather_rows(): pl.pallas_call(functools.partial(share, shards), out_shape=jax.ShapeDtype...  14 us
    gather x1, local copies, waits for them, and re-layouts, body(): wanted = lax.all_gather(targets[local], 'wide', axis=0)  3.13 us
  transfers between devices with their start and end apart: 1, of which 0 were waited for; matrix products, arithmetic and copies ran while one was open for 3% of the time, Pallas kernels for 38%

profile of v2, /device:TPU:0, one launch (start us, length us, event | category | flops | bytes accessed | tf_op | source)
XLA Modules:
  0.0 126.3 jit_solution(1698262106184647030)
XLA Ops:
  7.2 0.0 all-gather.3.cloned.1.call-start
  7.2 1.3 %fusion.3 = (s32[1]{0:T(128)}, s32[1]{0:T(128)}) fusion(s32[2]{0:T(128)} %param.6), kind=kLoop, calls=%fused_computation.9 | loop fusion | bytes 16 | tf_op jit(solution)/shard_map/slice | solution.py:302
  9.8 0.8 fusion.2
  10.6 0.1 fusion
  10.6 3.1 %gather_fusion.1 = f32[128,128]{1,0:T(8,128)} fusion(f32[6144,128]{1,0:T(8,128)} %targets.1, s32[1024]{0:T(1024)S(1)} %pad_clamp_fusion), kind=kCustom, calls=%fused_computation.1 | custom fusion | bytes 131584 | tf_op jit(solution)/shard_map/gather | solution.py:304
  13.8 0.0 all-gather.3.cloned.1.call-update
  13.8 2.1 %copy.6.features = f32[6144,64]{1,0:T(8,128)S(1)} copy(f32[6144,64]{0,1:T(8,128)} %param.4) | data formatting | bytes 3145728 | tf_op args[0]
  15.9 0.0 copy-start
  15.9 0.6 gather_fusion
  16.6 1.0 pad_maximum_fusion.x_ref
  17.6 14.0 %share_rows.1.shared = f32[16,64,128]{2,1,0:T(8,128)} custom-call(f32[64,128]{1,0:T(8,128)} %pad_maximum_fusion.x_ref), custom_call_target="tpu_custom_call" | custom-call | tf_op jit(solution)/shard_map/share_rows/pallas_call | solution.py:142
  31.5 33.5 %factor_blocks.1 = (bf16[2048,384]{1,0:T(8,128)(2,1)}, f32[8,2048]{1,0:T(8,128)}, f32[2,768,768]{2,1,0:T(8,128)}, f32[2,4,256,256]{3,2,1,0:T(8,128)}) custom-call(f32[16,64,128]{2,1,0:T(8,128)} %share_rows.1.shared), custom_call_target="tpu_custom_call" | custom-call | flops 51539607552 | bytes 16777216 | tf_op jit(solution)/shard_map/factor_blocks/pallas_call | solution.py:310
  65.0 0.0 copy-done
  66.2 0.6 pad_add_fusion.scalars
  66.8 0.0 all-gather.3.cloned.1.call-done
  66.9 52.7 %solve_and_update.1 = (f32[6144,128]{1,0:T(8,128)}, f32[6144,128]{1,0:T(8,128)}) custom-call(s32[130]{0:T(256)} %pad_add_fusion.scalars, f32[16,64,128]{2,1,0:T(8,128)} %share_rows.1.shared, f32[16,128,128]{2,1,0:T(8,128)} %bitcast.10, bf16[2048,384]{1,0:T(8,128)(2,1)} %get-tuple-element.6.right, f32[8,2048]{1,0:T(8,128)} %get-tuple-element.7.right_sq, ...), custom_call_target="tpu_custom_call" | custom-call | flops 4831838208 | bytes 11010048 | tf_op jit(solution)/shard_map/solve_and_update/pallas_call | solution.py:352
  (2 shorter events, 0.0 us)
Async XLA Ops:
  7.2 59.7 %all-gather.3.cloned.1.call-start = ((), (), s32[]{:S(2)}) async-start(), calls=%async_computation | async-start | bytes 1114112 | tf_op jit(solution)/shard_map/all_gather | solution.py:304
  15.9 49.1 %copy-start = (f32[6144,64]{1,0:T(8,128)}, f32[6144,64]{1,0:T(8,128)S(1)}, u32[]{:S(2)}) copy-start(f32[6144,64]{1,0:T(8,128)S(1)} %copy.6.features) | copy-start | bytes 4718596
Sparse Core Ops, SparseCore 0:
  13.9 40.7 all-gather.2

commit v3 on v2

--- a/solution.py
+++ b/solution.py
@@ -45,26 +45,38 @@
     return high, mid, low, first
 
 
+def norm_chunk(square, first_lane, other_lane, sign):
+    high = square.astype(BF16).astype(F32)
+    rest = square - high
+    mid = rest.astype(BF16).astype(F32)
+    lane = lax.broadcasted_iota(jnp.int32, (square.shape[0], 128), 1)
+    terms = jnp.where(lane == first_lane, high, jnp.where(lane == first_lane + 1, mid, rest - mid))
+    inside = (lane >= first_lane) & (lane < first_lane + 3)
+    other = (lane >= other_lane) & (lane < other_lane + 3)
+    return jnp.where(inside, sign * terms, jnp.where(other, 1.0 * sign, 0.0)).astype(BF16)
+
+
+def squares(x):
+    return jnp.sum(x * x, axis=1, keepdims=True) * (LOG2E / 32.0)
+
+
 def pack_left(x):
-    high, mid, low, first = parts3(x)
-    return jnp.concatenate(
-        [high.astype(BF16), mid.astype(BF16), jnp.where(first, high, low).astype(BF16)], axis=1
-    )
+    high, mid, low, first = parts3(x * (LOG2E / 16.0))
+    cross = jnp.where(first, high, low).astype(BF16)
+    norm = norm_chunk(squares(x), 0, 3, 1.0)
+    return jnp.concatenate([high.astype(BF16), mid.astype(BF16), cross, norm], axis=1)
 
 
 def pack_right(x):
     high, mid, low, first = parts3(x)
     both = jnp.where(first, high, mid).astype(BF16)
-    return jnp.concatenate([both, both, jnp.where(first, low, high).astype(BF16)], axis=1)
-
-
-def left_side(x):
-    return pack_left(x * (LOG2E / 16.0)), jnp.sum(x * x, axis=1, keepdims=True) * (LOG2E / 32.0)
-
-
-def gauss(left, left_sq, right, right_sq):
-    cross = lax.dot_general(left, right, NT, preferred_element_type=F32)
-    return jnp.exp2(cross - left_sq - right_sq)
+    cross = jnp.where(first, low, high).astype(BF16)
+    norm = norm_chunk(squares(x), 3, 0, -1.0)
+    return jnp.concatenate([both, both, cross, norm], axis=1)
+
+
+def gauss(left, right):
+    return jnp.exp2(lax.dot_general(left, right, NT, preferred_element_type=F32))
 
 
 def bounds_radius():
@@ -150,25 +162,23 @@
     )(x)
 
 
-def factor(shared, right, right_sq, weights, inverse, gram, power):
+def factor(shared, right, weights, inverse, gram, power):
     tiles = BLOCK // TILE
-    ones = jnp.ones((8, shared.shape[2] // STEPS), F32)
     for system in range(STEPS):
         for tile in range(tiles):
             x = feats_of(shared, system, tile)
             at = slice(system * BLOCK + tile * TILE, system * BLOCK + (tile + 1) * TILE)
             right[at, :] = pack_right(x)
-            right_sq[:, at] = full(ones, x * x, NT) * (LOG2E / 32.0)
     eye = (
         lax.broadcasted_iota(jnp.int32, (TILE, TILE), 0)
         == lax.broadcasted_iota(jnp.int32, (TILE, TILE), 1)
     ).astype(F32)
     for system in range(STEPS):
         for tile in range(tiles):
-            left, left_sq = left_side(feats_of(shared, system, tile))
+            left = pack_left(feats_of(shared, system, tile))
             for other in range(tile + 1):
                 at = slice(system * BLOCK + other * TILE, system * BLOCK + (other + 1) * TILE)
-                value = gauss(left, left_sq, right[at, :], right_sq[0:1, at])
+                value = gauss(left, right[at, :])
                 if other == tile:
                     value = value + 1.0 * eye
                 gram[system, span(tile), span(other)] = value
@@ -183,12 +193,11 @@
             square = rho * rho
             step = 2.0 / (2.0 - square)
             for system in range(STEPS):
-                e = split2(power[system])
                 x = inverse[system, k]
-                x_new = step * (x + three(split2(x), e))
-                e_new = (1.0 - step) * eye + step * three(e, e)
-                inverse[system, k] = x_new
-                power[system] = e_new
+                high, low = split2(jnp.concatenate([power[system], x], axis=0))
+                product = three((high, low), (high[0:TILE], low[0:TILE]))
+                inverse[system, k] = step * (x + product[TILE:])
+                power[system] = (1.0 - step) * eye + step * product[0:TILE]
             return square / (2.0 - square)
 
         lax.fori_loop(0, SQUARINGS, squaring, jnp.float32(radius))
@@ -210,7 +219,7 @@
                 )
 
 
-def solve(same, shared, wanted, right, right_sq, weights, inverse, rhs, delta):
+def solve(same, shared, wanted, right, weights, inverse, rhs, delta):
     tiles = BLOCK // TILE
     per = shared.shape[1]
     chunk = TILE // per
@@ -240,9 +249,9 @@
         backward(0, k)
     delta_one = split2(delta[0:BLOCK, :])
     for tile in range(tiles):
-        left, left_sq = left_side(feats_of(shared, 1, tile))
+        left = pack_left(feats_of(shared, 1, tile))
         at = slice(BLOCK + tile * TILE, BLOCK + (tile + 1) * TILE)
-        cross = gauss(left, left_sq, right[0:BLOCK, :], right_sq[0:1, 0:BLOCK])
+        cross = gauss(left, right[0:BLOCK, :])
         change = three(split2(cross), delta_one) + same * delta[tile * TILE : (tile + 1) * TILE, :]
         rhs[at, :] = rhs[at, :] - change
     for k in range(tiles):
@@ -252,7 +261,7 @@
 
 
 def update(
-    scalars, shared, wanted, right, right_sq, weights, inverse, features, targets,
+    scalars, shared, wanted, right, weights, inverse, features, targets,
     coeffs, residual, rhs, delta, packed,
 ):
     per = shared.shape[1]
@@ -263,7 +272,7 @@
     def _():
         me = scalars[STEPS * per]
         same = scalars[STEPS * per + 1].astype(F32)
-        solve(same, shared, wanted, right, right_sq, weights, inverse, rhs, delta)
+        solve(same, shared, wanted, right, weights, inverse, rhs, delta)
         high, low = split2(delta[...])
         packed[...] = jnp.concatenate([high, low], axis=1)
         coeffs[...] = jnp.zeros_like(coeffs)
@@ -277,12 +286,12 @@
 
             lax.fori_loop(0, per, put, 0)
 
-    left, left_sq = left_side(features[...])
+    left = pack_left(features[...])
     width = 512
     total = jnp.zeros((rows, 128), F32)
     for at in range(0, STEPS * BLOCK, width):
         cols = slice(at, at + width)
-        value = gauss(left, left_sq, right[cols, :], right_sq[0:1, cols])
+        value = gauss(left, right[cols, :])
         high, low = split2(value)
         wide = jnp.dot(high, packed[cols, :], preferred_element_type=F32)
         narrow = jnp.dot(low, packed[cols, 0:128], preferred_element_type=F32)
@@ -307,11 +316,10 @@
     same = (block_ids[0] == block_ids[1]).astype(jnp.int32)
     scalars = jnp.concatenate([local, jnp.stack([me, same])])
     limit = pltpu.CompilerParams(vmem_limit_bytes=56 * 1024 * 1024)
-    right, right_sq, weights, inverse = pl.pallas_call(
+    right, weights, inverse = pl.pallas_call(
         factor,
         out_shape=[
-            jax.ShapeDtypeStruct((STEPS * BLOCK, 6 * feat), BF16),
-            jax.ShapeDtypeStruct((8, STEPS * BLOCK), F32),
+            jax.ShapeDtypeStruct((STEPS * BLOCK, 8 * feat), BF16),
             jax.ShapeDtypeStruct((STEPS, BLOCK - TILE, BLOCK - TILE), F32),
             jax.ShapeDtypeStruct((STEPS, tiles, TILE, TILE), F32),
         ],
@@ -330,7 +338,7 @@
     def whole(array):
         return pl.BlockSpec(array.shape, lambda i, s: (0,) * array.ndim)
 
-    fixed = (shared, wanted, right, right_sq, weights, inverse)
+    fixed = (shared, wanted, right, weights, inverse)
     grid_spec = pltpu.PrefetchScalarGridSpec(
         num_scalar_prefetch=1,
         grid=(rows_dev // tile,),

time: 127 us -> 128 us (level)
    pallas_call x1, Pallas kernels: 33.5 us -> 36.5 us  [body(): pl.pallas_call(factor, out_shape=[jax.ShapeDtypeStruct((STEPS * BLOCK, 8...]
    pallas_call x1, Pallas kernels: 52.7 us -> 50.3 us  [body(): pl.pallas_call(update, grid_spec=grid_spec, out_shape=[jax.ShapeDtypeStru...]
  transfers between devices with their start and end apart: 1 -> 1, of which waited for: 0 -> 0; matrix products, arithmetic and copies ran while one was open for 3% -> 3% of each run, Pallas kernels for 38% -> 40%
where the time goes in v3:
time: 128 us; the launch traced here: 127 us
  Pallas kernels  101 us (79%)
  between operations  16.5 us (13%)
  local copies, waits for them, and re-layouts  8.01 us (6%)
  other arithmetic  1.68 us (1%)
    pallas_call x1, Pallas kernels, body(): pl.pallas_call(update, grid_spec=grid_spec, out_shape=[jax.ShapeDtypeStru...  50.3 us
    pallas_call x1, Pallas kernels, body(): pl.pallas_call(factor, out_shape=[jax.ShapeDtypeStruct((STEPS * BLOCK, 8...  36.5 us
    pallas_call x1, Pallas kernels, gather_rows(): pl.pallas_call(functools.partial(share, shards), out_shape=jax.ShapeDtype...  14 us
    gather x1, local copies, waits for them, and re-layouts, body(): wanted = lax.all_gather(targets[local], 'wide', axis=0)  3.13 us
  transfers between devices with their start and end apart: 1, of which 0 were waited for; matrix products, arithmetic and copies ran while one was open for 3% of the time, Pallas kernels for 40%

profile of v3, /device:TPU:0, one launch (start us, length us, event | category | flops | bytes accessed | tf_op | source)
XLA Modules:
  0.0 127.1 jit_solution(4927721689855621755)
XLA Ops:
  7.2 0.0 all-gather.3.cloned.1.call-start
  7.2 1.3 %fusion.3 = (s32[1]{0:T(128)}, s32[1]{0:T(128)}) fusion(s32[2]{0:T(128)} %param.6), kind=kLoop, calls=%fused_computation.9 | loop fusion | bytes 16 | tf_op jit(solution)/shard_map/slice | solution.py:311
  9.8 0.8 fusion.2
  10.6 0.1 fusion
  10.6 3.1 %gather_fusion.1 = f32[128,128]{1,0:T(8,128)} fusion(f32[6144,128]{1,0:T(8,128)} %targets.1, s32[1024]{0:T(1024)S(1)} %pad_clamp_fusion), kind=kCustom, calls=%fused_computation.1 | custom fusion | bytes 131584 | tf_op jit(solution)/shard_map/gather | solution.py:313
  13.8 0.0 all-gather.3.cloned.1.call-update
  13.8 2.1 %copy.6.features = f32[6144,64]{1,0:T(8,128)S(1)} copy(f32[6144,64]{0,1:T(8,128)} %param.4) | data formatting | bytes 3145728 | tf_op args[0]
  15.9 0.0 copy-start
  15.9 0.6 gather_fusion
  16.6 1.0 pad_maximum_fusion.x_ref
  17.6 14.0 %share_rows.1.shared = f32[16,64,128]{2,1,0:T(8,128)} custom-call(f32[64,128]{1,0:T(8,128)} %pad_maximum_fusion.x_ref), custom_call_target="tpu_custom_call" | custom-call | tf_op jit(solution)/shard_map/share_rows/pallas_call | solution.py:154
  31.5 36.5 %factor_blocks.1 = (bf16[2048,512]{1,0:T(8,128)(2,1)}, f32[2,768,768]{2,1,0:T(8,128)}, f32[2,4,256,256]{3,2,1,0:T(8,128)}) custom-call(f32[16,64,128]{2,1,0:T(8,128)} %share_rows.1.shared), custom_call_target="tpu_custom_call" | custom-call | flops 51539607552 | bytes 16777216 | tf_op jit(solution)/shard_map/factor_blocks/pallas_call | solution.py:319
  68.1 0.0 copy-done
  69.3 0.6 pad_add_fusion.scalars
  69.9 0.0 all-gather.3.cloned.1.call-done
  69.9 50.3 %solve_and_update.1 = (f32[6144,128]{1,0:T(8,128)}, f32[6144,128]{1,0:T(8,128)}) custom-call(s32[130]{0:T(256)} %pad_add_fusion.scalars, f32[16,64,128]{2,1,0:T(8,128)} %share_rows.1.shared, f32[16,128,128]{2,1,0:T(8,128)} %bitcast.10, bf16[2048,512]{1,0:T(8,128)(2,1)} %get-tuple-element.5.right, f32[2,768,768]{2,1,0:T(8,128)} %get-tuple-element.6.weights, ...), custom_call_target="tpu_custom_call" | custom-call | flops 4831838208 | bytes 11010048 | tf_op jit(solution)/shard_map/solve_and_update/pallas_call | solution.py:360
  (2 shorter events, 0.0 us)
Async XLA Ops:
  7.2 62.7 %all-gather.3.cloned.1.call-start = ((), (), s32[]{:S(2)}) async-start(), calls=%async_computation | async-start | bytes 1114112 | tf_op jit(solution)/shard_map/all_gather | solution.py:313
  15.9 52.2 %copy-start = (f32[6144,64]{1,0:T(8,128)}, f32[6144,64]{1,0:T(8,128)S(1)}, u32[]{:S(2)}) copy-start(f32[6144,64]{1,0:T(8,128)S(1)} %copy.6.features) | copy-start | bytes 4718596
Sparse Core Ops, SparseCore 0:
  13.9 40.6 all-gather.2
